TPU v7x, 512 devices: a whole 4x4x16 slice. The times are simulated.
512 devices in a mesh: tm: 32 (over x, y, core), tile: 16 (over z).
Axes of the slice: x: 4, y: 4, z: 16, core: 2. Of those that a mesh axis runs over, the one named last changes fastest.
Arguments:
- seg_gain: bfloat16 [32, 1024, 1024], P('tm', 'tile'), may hold values from -0.1875 to 0.1875
- seg_offset: float32 [32, 1024], P('tm', 'tile'), may hold values from -6 to 6
- seg_noise: bfloat16 [32, 1024, 1024], P('tm', 'tile'), as said below
- end_mean: bfloat16 [8, 1024], P(None, 'tile'), may hold values from -6 to 6
- end_cov: bfloat16 [8, 1024, 1024], P(None, 'tile'), as said below
- step_gain: bfloat16 [256, 1024, 1024], P('tm', 'tile'), may hold values from -0.1875 to 0.1875
- step_offset: float32 [256, 1024], P('tm', 'tile'), may hold values from -6 to 6
- step_var: float32 [256, 1024], P('tm', 'tile'), may hold values from 0.1 to 1.5
- obs_tiles: int32 [256, 4], P('tm'), may hold values from 0 to 7
- obs_count: int32 [256], P('tm'), may hold values from 1 to 4, as said below
- obs_value: float32 [256, 4, 128], P('tm'), may hold values from -10 to 10
- obs_noise: float32 [1024], replicated, may hold values from 0.2 to 2
Outputs:
- start_cov: bfloat16 [32, 1024, 1024], P('tm', 'tile')
- start_mean: bfloat16 [32, 1024], P('tm', 'tile')
- step_mean: float32 [256, 1024], P('tm', 'tile')
- step_spread: float32 [256, 1024], P('tm', 'tile')
- innovation: float32 [256, 4, 128], P('tm')
Inputs may be any that keep to these rules, and one draw needn't show every extreme that they name: `end_cov`: each matrix is symmetric and positive definite. `seg_noise`: each matrix is symmetric and positive definite. `obs_count`: some step has 4 live slots and some has 1.
All inputs are finite; a program needn't handle non-finite values.
Results may differ from a plain program's by a relative error of at most 0.015.
Values may be sent and summed in bfloat16 or wider, within the bound.
A program may use at most 64 MiB of HBM per device.

v0:
```python
import jax
import jax.numpy as jnp
from jax import lax
from jax.sharding import PartitionSpec as P

TILE_STATES = 128
SLOTS = 4
GROUP_SEGS = 4


def shifted(block, axis, distance):
    devices = range(lax.axis_size(axis))
    route = [(i - distance, i) for i in devices if i - distance in devices]
    return lax.ppermute(block, axis, route)


def shards(
    seg_gain,
    seg_offset,
    seg_noise,
    end_mean,
    end_cov,
    step_gain,
    step_offset,
    step_var,
    obs_tiles,
    obs_count,
    obs_value,
    obs_noise,
):
    position = lax.axis_index("tm")
    slot_place = position % GROUP_SEGS
    group_index = position // GROUP_SEGS
    gain_rows = seg_gain[0]
    offset_rows = seg_offset[0]
    noise_rows = seg_noise[0].astype(jnp.float32)
    row_count = gain_rows.shape[0]
    state_count = gain_rows.shape[1]
    cur_mean = lax.dynamic_index_in_dim(end_mean, group_index, 0, keepdims=False)
    cur_cov = lax.dynamic_index_in_dim(end_cov, group_index, 0, keepdims=False)
    kept_mean = jnp.zeros((state_count,), jnp.bfloat16)
    kept_cov = jnp.zeros((state_count, state_count), jnp.bfloat16)
    out_mean = jnp.zeros((row_count,), jnp.bfloat16)
    out_cov = jnp.zeros((row_count, state_count), jnp.bfloat16)
    for depth_step in range(GROUP_SEGS):
        whole_mean, whole_cov = (
            lax.all_gather(cur_mean, "tile", axis=0, tiled=True),
            lax.all_gather(cur_cov, "tile", axis=0, tiled=True),
        )
        is_mine = slot_place == GROUP_SEGS - 1 - depth_step
        kept_mean = jnp.where(is_mine, whole_mean, kept_mean)
        kept_cov = jnp.where(is_mine, whole_cov, kept_cov)
        product = jnp.dot(gain_rows, whole_cov, preferred_element_type=jnp.float32).astype(
            jnp.bfloat16
        )
        col_block = jnp.einsum(
            "pd,rd->pr",
            lax.all_gather(product, "tile", axis=0, tiled=True),
            gain_rows,
            preferred_element_type=jnp.float32,
        )
        spread_rows = lax.all_to_all(col_block, "tile", split_axis=0, concat_axis=1, tiled=True)
        new_cov = (spread_rows + noise_rows).astype(jnp.bfloat16)
        new_mean = (
            jnp.dot(gain_rows, whole_mean, preferred_element_type=jnp.float32) + offset_rows
        ).astype(jnp.bfloat16)
        out_mean = jnp.where(is_mine, new_mean, out_mean)
        out_cov = jnp.where(is_mine, new_cov, out_cov)
        if depth_step < GROUP_SEGS - 1:
            got_mean, got_cov = shifted((new_mean, new_cov), "tm", -1)
            takes_next = slot_place == GROUP_SEGS - 2 - depth_step
            cur_mean = jnp.where(takes_next, got_mean, cur_mean)
            cur_cov = jnp.where(takes_next, got_cov, cur_cov)
    partial_value = jnp.einsum(
        "krd,de->kre", step_gain, kept_cov, preferred_element_type=jnp.float32
    )
    local_spread = jnp.sum(partial_value * step_gain, axis=2) + step_var
    local_mean = (
        jnp.einsum("krd,d->kr", step_gain, kept_mean, preferred_element_type=jnp.float32)
        + step_offset
    )
    full_mean, full_spread = (
        lax.all_gather(local_mean, "tile", axis=1, tiled=True),
        lax.all_gather(local_spread, "tile", axis=1, tiled=True),
    )
    step_count = full_mean.shape[0]
    tile_total = state_count // TILE_STATES
    tile_mean = full_mean.reshape(step_count, tile_total, TILE_STATES)
    tile_spread = full_spread.reshape(step_count, tile_total, TILE_STATES) + obs_noise.reshape(
        1, tile_total, TILE_STATES
    )
    onehot = (
        obs_tiles[:, :, None] == jnp.arange(tile_total, dtype=jnp.int32)[None, None, :]
    ).astype(jnp.float32)
    picked_mean = jnp.einsum("ksn,kno->kso", onehot, tile_mean, precision=lax.Precision.HIGHEST)
    picked_spread = jnp.einsum("ksn,kno->kso", onehot, tile_spread, precision=lax.Precision.HIGHEST)
    live_slots = jnp.arange(SLOTS, dtype=jnp.int32)[None, :] < obs_count[:, None]
    innovation = jnp.where(
        live_slots[:, :, None], (obs_value - picked_mean) / picked_spread, jnp.float32(0.0)
    )
    return (out_cov[None], out_mean[None], local_mean, local_spread, innovation)


def solution(mesh):
    in_specs = (
        P("tm", "tile", None),
        P("tm", "tile"),
        P("tm", "tile", None),
        P(None, "tile"),
        P(None, "tile", None),
        P("tm", "tile", None),
        P("tm", "tile"),
        P("tm", "tile"),
        P("tm", None),
        P("tm"),
        P("tm", None, None),
        P(),
    )
    out_specs = (
        P("tm", "tile", None),
        P("tm", "tile"),
        P("tm", "tile"),
        P("tm", "tile"),
        P("tm", None, None),
    )
    return jax.shard_map(shards, mesh=mesh, in_specs=in_specs, out_specs=out_specs, check_vma=False)
```

profile of v0, /device:TPU:2, one launch (start us, length us, event | category | flops | bytes accessed | tf_op | source)
XLA Modules:
  0.0 827.4 jit_solution(18395162919575817385)
XLA Ops:
  8.9 79.4 %all-gather.27.cloned.1.call-done = bf16[1,1024,1024]{2,1,0:T(8,128)(2,1)} async-done(((bf16[1,64,1024]{2,1,0:T(8,128)(2,1)}), bf16[1,1024,1024]{2,1,0:T(8,128)(2,1)}) %all-gather.27.cloned.1.call-update) | async-done | bytes 2097168 | tf_op jit(solution)/shard_map/all_gather | solution.py:48
  88.3 2.7 fusion.19
  91.1 70.2 %all-gather.13.cloned.1.call-done = bf16[1024,1024]{1,0:T(8,128)(2,1)} async-done(((bf16[64,1024]{1,0:T(8,128)(2,1)}), bf16[1024,1024]{1,0:T(8,128)(2,1)}) %all-gather.13.cloned.1.call-update) | async-done | bytes 2097168 | tf_op jit(solution)/shard_map/all_gather | solution.py:58
  161.2 2.3 fusion.56
  163.9 21.7 %all_to_all.73 = f32[16,1,4096]{2,1,0:T(1,128)S(1)} all-to-all(f32[16,1,4096]{2,1,0:T(1,128)S(1)} %reshape.104), channel_id=1, replica_groups=mesh['tm'=32,'tile'=16] {'tile'}, dimensions={0} | all-to-all | bytes 524288 | tf_op jit(solution)/shard_map/all_to_all | solution.py:62
  189.9 2.5 collective-permute-done
  194.1 69.4 %all-gather.15.cloned.1.call-done = bf16[1024,1024]{1,0:T(8,128)(2,1)} async-done(((bf16[64,1024]{1,0:T(8,128)(2,1)}), bf16[1024,1024]{1,0:T(8,128)(2,1)}) %all-gather.15.cloned.1.call-update) | async-done | bytes 2097168 | tf_op jit(solution)/shard_map/all_gather | solution.py:48
  263.5 2.7 fusion.16
  266.3 70.3 %all-gather.17.cloned.1.call-done = bf16[1024,1024]{1,0:T(8,128)(2,1)} async-done(((bf16[64,1024]{1,0:T(8,128)(2,1)}), bf16[1024,1024]{1,0:T(8,128)(2,1)}) %all-gather.17.cloned.1.call-update) | async-done | bytes 2097168 | tf_op jit(solution)/shard_map/all_gather | solution.py:58
  336.6 2.3 fusion.54
  339.2 21.8 %all_to_all.74 = f32[16,1,4096]{2,1,0:T(1,128)S(1)} all-to-all(f32[16,1,4096]{2,1,0:T(1,128)S(1)} %reshape.106), channel_id=1, replica_groups=mesh['tm'=32,'tile'=16] {'tile'}, dimensions={0} | all-to-all | bytes 524288 | tf_op jit(solution)/shard_map/all_to_all | solution.py:62
  364.8 2.5 collective-permute-done.1
  368.1 69.4 %all-gather.19.cloned.1.call-done = bf16[1024,1024]{1,0:T(8,128)(2,1)} async-done(((bf16[64,1024]{1,0:T(8,128)(2,1)}), bf16[1024,1024]{1,0:T(8,128)(2,1)}) %all-gather.19.cloned.1.call-update) | async-done | bytes 2097168 | tf_op jit(solution)/shard_map/all_gather | solution.py:48
  437.5 2.7 fusion.17
  440.3 70.3 %all-gather.21.cloned.1.call-done = bf16[1024,1024]{1,0:T(8,128)(2,1)} async-done(((bf16[64,1024]{1,0:T(8,128)(2,1)}), bf16[1024,1024]{1,0:T(8,128)(2,1)}) %all-gather.21.cloned.1.call-update) | async-done | bytes 2097168 | tf_op jit(solution)/shard_map/all_gather | solution.py:58
  510.6 2.3 fusion.52
  513.2 21.8 %all_to_all.75 = f32[16,1,4096]{2,1,0:T(1,128)S(1)} all-to-all(f32[16,1,4096]{2,1,0:T(1,128)S(1)} %reshape.108), channel_id=1, replica_groups=mesh['tm'=32,'tile'=16] {'tile'}, dimensions={0} | all-to-all | bytes 524288 | tf_op jit(solution)/shard_map/all_to_all | solution.py:62
  538.9 2.5 collective-permute-done.2
  542.2 69.4 %all-gather.23.cloned.1.call-done = bf16[1024,1024]{1,0:T(8,128)(2,1)} async-done(((bf16[64,1024]{1,0:T(8,128)(2,1)}), bf16[1024,1024]{1,0:T(8,128)(2,1)}) %all-gather.23.cloned.1.call-update) | async-done | bytes 2097168 | tf_op jit(solution)/shard_map/all_gather | solution.py:48
  611.6 2.7 fusion.18
  616.6 29.9 %all-reduce = bf16[1024]{0:T(1024)(128)(2,1)S(1)} all-reduce(bf16[1024]{0:T(1024)(128)(2,1)S(1)} %dynamic-update-slice), channel_id=3, replica_groups=mesh['tm'=32,'tile'=16] {'tile'}, use_global_device_ids=true, to_apply=%add | all-reduce | flops 1024 | bytes 4096 | tf_op jit(solution)/shard_map/all_gather | solution.py:47
  646.7 1.9 collective-permute-start.3
  650.1 27.1 %all-reduce.1 = bf16[1024]{0:T(1024)(128)(2,1)S(1)} all-reduce(bf16[1024]{0:T(1024)(128)(2,1)S(1)} %dynamic-update-slice.1), channel_id=1, replica_groups=mesh['tm'=32,'tile'=16] {'tile'}, use_global_device_ids=true, to_apply=%add.1 | all-reduce | flops 1024 | bytes 4096
  677.3 1.9 collective-permute-start.4
  680.8 29.1 %all-reduce.2 = bf16[1024]{0:T(1024)(128)(2,1)S(1)} all-reduce(bf16[1024]{0:T(1024)(128)(2,1)S(1)} %dynamic-update-slice.2), channel_id=1, replica_groups=mesh['tm'=32,'tile'=16] {'tile'}, use_global_device_ids=true, to_apply=%add.2 | all-reduce | flops 1024 | bytes 4096
  710.0 1.9 collective-permute-start.5
  713.4 27.2 %all-reduce.3 = bf16[1024]{0:T(1024)(128)(2,1)S(1)} all-reduce(bf16[1024]{0:T(1024)(128)(2,1)S(1)} %dynamic-update-slice.3), channel_id=1, replica_groups=mesh['tm'=32,'tile'=16] {'tile'}, use_global_device_ids=true, to_apply=%add.3 | all-reduce | flops 1024 | bytes 4096
  742.5 28.3 %all-gather.2 = f32[16,64,8]{1,2,0:T(8,128)S(1)} all-gather(f32[1,64,8]{1,2,0:T(8,128)S(1)} %bitcast.172), channel_id=1, replica_groups=mesh['tm'=32,'tile'=16] {'tile'}, dimensions={0}, use_global_device_ids=true | all-gather | bytes 34816 | tf_op jit(solution)/shard_map/all_gather | solution.py:83
  773.0 2.4 fusion.50
  776.4 6.6 all-to-all-start.3
  783.0 3.8 fusion
  786.8 30.1 %all-gather.3 = f32[16,64,8]{1,2,0:T(8,128)S(1)} all-gather(f32[1,64,8]{1,2,0:T(8,128)S(1)} %bitcast.173), channel_id=1, replica_groups=mesh['tm'=32,'tile'=16] {'tile'}, dimensions={0}, use_global_device_ids=true | all-gather | bytes 34816 | tf_op jit(solution)/shard_map/all_gather | solution.py:84
  (122 shorter events, 33.0 us)
Async XLA Ops:
  7.2 81.1 %copy-start = (bf16[1,64,1024]{2,1,0:T(8,128)(2,1)S(1)}, bf16[1,64,1024]{2,1,0:T(8,128)(2,1)}, u32[]{:S(2)}) copy-start(bf16[1,64,1024]{2,1,0:T(8,128)(2,1)} %param.12) | copy-start | bytes 393220
  7.2 81.1 %all-gather.27.cloned.1.call-start = ((), (), s32[]{:S(2)}) async-start(), calls=%async_computation.11 | async-start | bytes 2228224 | tf_op jit(solution)/shard_map/all_gather | solution.py:48
  8.8 152.4 %all-gather.13.cloned.1.call-start = ((), (), s32[]{:S(2)}) async-start(), calls=%async_computation.4 | async-start | bytes 2228224 | tf_op jit(solution)/shard_map/all_gather | solution.py:58
  91.0 172.5 %all-gather.15.cloned.1.call-start = ((), (), s32[]{:S(2)}) async-start(), calls=%async_computation.5 | async-start | bytes 2228224 | tf_op jit(solution)/shard_map/all_gather | solution.py:48
  163.5 24.4 %copy-start.2 = (bf16[1,64,1024]{2,1,0:T(8,128)(2,1)S(1)}, bf16[1,64,1024]{2,1,0:T(8,128)(2,1)}, u32[]{:S(2)}) copy-start(bf16[1,64,1024]{2,1,0:T(8,128)(2,1)} %param.14) | copy-start | bytes 393220
  188.0 4.4 collective-permute-start
  194.0 142.6 %all-gather.17.cloned.1.call-start = ((), (), s32[]{:S(2)}) async-start(), calls=%async_computation.6 | async-start | bytes 2228224 | tf_op jit(solution)/shard_map/all_gather | solution.py:58
  266.2 171.3 %all-gather.19.cloned.1.call-start = ((), (), s32[]{:S(2)}) async-start(), calls=%async_computation.7 | async-start | bytes 2228224 | tf_op jit(solution)/shard_map/all_gather | solution.py:48
  339.2 28.2 %copy-start.3 = (bf16[64,1024]{1,0:T(8,128)(2,1)S(1)}, bf16[64,1024]{1,0:T(8,128)(2,1)}, u32[]{:S(2)}) copy-start(bf16[64,1024]{1,0:T(8,128)(2,1)} %bitcast_select_fusion.1) | copy-start | bytes 393220
  362.9 4.4 collective-permute-start.1
  368.0 142.6 %all-gather.21.cloned.1.call-start = ((), (), s32[]{:S(2)}) async-start(), calls=%async_computation.8 | async-start | bytes 2228224 | tf_op jit(solution)/shard_map/all_gather | solution.py:58
  440.3 171.3 %all-gather.23.cloned.1.call-start = ((), (), s32[]{:S(2)}) async-start(), calls=%async_computation.9 | async-start | bytes 2228224 | tf_op jit(solution)/shard_map/all_gather | solution.py:48
  513.2 28.2 %copy-start.4 = (bf16[64,1024]{1,0:T(8,128)(2,1)S(1)}, bf16[64,1024]{1,0:T(8,128)(2,1)}, u32[]{:S(2)}) copy-start(bf16[64,1024]{1,0:T(8,128)(2,1)} %broadcast_select_fusion) | copy-start | bytes 393220
  536.8 79.6 %copy-start.12 = (bf16[8,64]{1,0:T(8,128)(2,1)S(1)}, bf16[8,64]{1,0:T(8,128)(2,1)}, u32[]{:S(2)}) copy-start(bf16[8,64]{1,0:T(8,128)(2,1)} %param.15) | copy-start | bytes 3076
  536.8 109.8 %copy-start.15 = (f32[1,64]{1,0:T(1,128)S(1)}, f32[1,64]{1,0:T(1,128)}, u32[]{:S(2)}) copy-start(f32[1,64]{1,0:T(1,128)} %param.13) | copy-start | bytes 772
  537.0 142.3 %copy-start.14 = (s32[8]{0:T(128)S(1)}, s32[8]{0:T(128)}, u32[]{:S(2)}) copy-start(s32[8]{0:T(128)} %param.21) | copy-start | bytes 100
  537.0 175.0 %copy-start.11 = (s32[8,4]{0,1:T(4,128)S(1)}, s32[8,4]{0,1:T(4,128)}, u32[]{:S(2)}) copy-start(s32[8,4]{0,1:T(4,128)} %param.20) | copy-start | bytes 388
  537.0 4.4 collective-permute-start.2
  542.1 200.3 %copy-start.9 = (f32[8,64]{1,0:T(8,128)S(1)}, f32[8,64]{1,0:T(8,128)}, u32[]{:S(2)}) copy-start(f32[8,64]{1,0:T(8,128)} %param.18) | copy-start | bytes 6148
  542.1 229.4 %copy-start.6 = (f32[8,4,128]{2,1,0:T(4,128)S(1)}, f32[8,4,128]{2,1,0:T(4,128)}, u32[]{:S(2)}) copy-start(f32[8,4,128]{2,1,0:T(4,128)} %param.22) | copy-start | bytes 49156
  542.1 230.8 %all-gather.25.cloned.1.call-start = ((), (), s32[]{:S(2)}) async-start(), calls=%async_computation.10 | async-start | bytes 2228224 | tf_op jit(solution)/shard_map/all_gather | solution.py:58
  646.7 3.2 collective-permute-start.3
  677.3 3.2 collective-permute-start.4
  710.0 3.2 collective-permute-start.5
  742.4 32.9 %copy-start.7 = (f32[8,64]{1,0:T(8,128)}, f32[8,64]{1,0:T(8,128)S(1)}, u32[]{:S(2)}) copy-start(f32[8,64]{1,0:T(8,128)S(1)} %add.74) | copy-start | bytes 6148
  772.9 10.1 %copy-start.1 = (bf16[1,1024,1024]{2,1,0:T(8,128)(2,1)S(1)}, bf16[1,1024,1024]{2,1,0:T(8,128)(2,1)}, u32[]{:S(2)}) copy-start(bf16[1,1024,1024]{2,1,0:T(8,128)(2,1)} %all-gather.27.cloned.1.call-done) | copy-start | bytes 6291460
  776.4 41.5 %all-to-all-start.3 = ((f32[16,1,4096]{2,1,0:T(1,128)}), f32[16,1,4096]{2,1,0:T(1,128)S(1)}, u32[]{:S(2)}, u32[]{:S(2)}) async-start(f32[16,1,4096]{2,1,0:T(1,128)} %reshape.110), calls=%async_computation.3 | async-start | bytes 524288 | tf_op jit(solution)/shard_map/all_to_all | solution.py:62
  783.0 3.8 copy-start.10
  783.0 34.0 %copy-start.13 = (f32[1024]{0:T(1024)S(1)}, f32[1024]{0:T(1024)}, u32[]{:S(2)}) copy-start(f32[1024]{0:T(1024)} %param.23) | copy-start | bytes 12292
  786.8 33.0 %copy-start.5 = (f32[1,64,1024]{2,1,0:T(8,128)S(1)}, f32[1,64,1024]{2,1,0:T(8,128)}, u32[]{:S(2)}) copy-start(f32[1,64,1024]{2,1,0:T(8,128)} %all_to_all.66) | copy-start | bytes 786436
  786.8 33.7 %copy-start.8 = (f32[8,64]{1,0:T(8,128)}, f32[8,64]{1,0:T(8,128)S(1)}, u32[]{:S(2)}) copy-start(f32[8,64]{1,0:T(8,128)S(1)} %add.75) | copy-start | bytes 6148
Sparse Core Ops, SparseCore 0:
  10.7 77.5 all-gather.26
  91.1 70.0 all-gather.12
  194.1 69.3 all-gather.14
  266.4 70.1 all-gather.16
  368.2 69.3 all-gather.18
  440.4 70.1 all-gather.20
  542.3 69.3 all-gather.22
  614.5 70.5 all-gather.24
where the time goes:
time: 828 us; the launch traced here: 827 us
  waiting for transfers between devices  510 us (62%)
  blocking collectives  237 us (29%)
  matrix products  27.8 us (3%)
  starting transfers between devices  18.4 us (2%)
  between operations  15.3 us (2%)
  local copies, waits for them, and re-layouts  10.7 us (1%)
  other arithmetic  8.55 us (1%)
    all_gather x4, waiting for transfers between devices, shards(): lax.all_gather(cur_cov, 'tile', axis=0, tiled=True)  288 us
    all_gather x4, waiting for transfers between devices, shards(): lax.all_gather(product, 'tile', axis=0, tiled=True)  211 us
    unnamed x3, blocking collectives  83.4 us
    all_to_all x3, blocking collectives, shards(): lax.all_to_all(col_block, 'tile', split_axis=0, concat_axis=1, tiled=True)  65.3 us
    all_gather x1, blocking collectives, shards(): lax.all_gather(local_spread, 'tile', axis=1, tiled=True)  30.1 us
    all_gather x1, blocking collectives, shards(): lax.all_gather(cur_mean, 'tile', axis=0, tiled=True)  29.9 us
    all_gather x1, blocking collectives, shards(): lax.all_gather(local_mean, 'tile', axis=1, tiled=True)  28.3 us
  transfers between devices with their start and end apart: 15, of which 13 were waited for; matrix products, arithmetic and copies ran while one was open for 1% of the time, Pallas kernels for 0%

commit v1 on v0

--- a/solution.py
+++ b/solution.py
@@ -6,6 +6,12 @@
 TILE_STATES = 128
 SLOTS = 4
 GROUP_SEGS = 4
+
+
+def gather_by_exchange(x, axis, dim):
+    devices = lax.axis_size(axis)
+    repeats = [devices if d == dim else 1 for d in range(x.ndim)]
+    return lax.all_to_all(jnp.tile(x, repeats), axis, split_axis=dim, concat_axis=dim, tiled=True)
 
 
 def shifted(block, axis, distance):
@@ -45,7 +51,7 @@
     for depth_step in range(GROUP_SEGS):
         whole_mean, whole_cov = (
             lax.all_gather(cur_mean, "tile", axis=0, tiled=True),
-            lax.all_gather(cur_cov, "tile", axis=0, tiled=True),
+            gather_by_exchange(cur_cov, "tile", 0),
         )
         is_mine = slot_place == GROUP_SEGS - 1 - depth_step
         kept_mean = jnp.where(is_mine, whole_mean, kept_mean)

time: 828 us -> 975 us (1.18)
  blocking collectives: 237 us -> 651 us
  waiting for transfers between devices: 510 us -> 227 us
  local copies, waits for them, and re-layouts: 10.7 us -> 27.8 us
    all_to_all x0 -> x4, blocking collectives: none -> 412 us  [gather_by_exchange(): lax.all_to_all(jnp.tile(x, repeats), axis, split_axis=dim, concat_axis=di...]
    all_gather x4 -> x0, waiting for transfers between devices: 288 us -> none  [shards(): lax.all_gather(cur_cov, 'tile', axis=0, tiled=True)]
  transfers between devices with their start and end apart: 15 -> 11, of which waited for: 13 -> 9; matrix products, arithmetic and copies ran while one was open for 1% -> 1% of each run, Pallas kernels for 0% -> 0%
where the time goes in v1:
time: 975 us; the launch traced here: 973 us
  blocking collectives  651 us (67%)
  waiting for transfers between devices  227 us (23%)
  local copies, waits for them, and re-layouts  27.8 us (3%)
  matrix products  22.1 us (2%)
  starting transfers between devices  17.4 us (2%)
  between operations  14.9 us (2%)
  other arithmetic  12.6 us (1%)
    all_to_all x4, blocking collectives, gather_by_exchange(): lax.all_to_all(jnp.tile(x, repeats), axis, split_axis=dim, concat_axis=di...  412 us
    all_gather x4, waiting for transfers between devices, shards(): lax.all_gather(product, 'tile', axis=0, tiled=True)  215 us
    unnamed x3, blocking collectives  83.1 us
    all_to_all x3, blocking collectives, shards(): lax.all_to_all(col_block, 'tile', split_axis=0, concat_axis=1, tiled=True)  65.6 us
    all_gather x1, blocking collectives, shards(): lax.all_gather(cur_mean, 'tile', axis=0, tiled=True)  32 us
    all_gather x1, blocking collectives, shards(): lax.all_gather(local_spread, 'tile', axis=1, tiled=True)  30.1 us
    all_gather x1, blocking collectives, shards(): lax.all_gather(local_mean, 'tile', axis=1, tiled=True)  28.3 us
  transfers between devices with their start and end apart: 11, of which 9 were waited for; matrix products, arithmetic and copies ran while one was open for 1% of the time, Pallas kernels for 0%

profile of v1, /device:TPU:2, one launch (start us, length us, event | category | flops | bytes accessed | tf_op | source)
XLA Modules:
  0.0 973.3 jit_solution(8329140792882046638)
XLA Ops:
  8.4 111.5 %all_to_all.109 = bf16[16,64,1024]{2,1,0:T(8,128)(2,1)S(1)} all-to-all(bf16[16,64,1024]{2,1,0:T(8,128)(2,1)S(1)} %tile.11), channel_id=1, replica_groups=mesh['tm'=32,'tile'=16] {'tile'}, dimensions={0} | all-to-all | bytes 4194304 | tf_op jit(solution)/shard_map/all_to_all | solution.py:14
  121.1 68.8 %all-gather.8.cloned.1.call-done = bf16[1024,1024]{1,0:T(8,128)(2,1)} async-done(((bf16[64,1024]{1,0:T(8,128)(2,1)}), bf16[1024,1024]{1,0:T(8,128)(2,1)}) %all-gather.8.cloned.1.call-update) | async-done | bytes 2097168 | tf_op jit(solution)/shard_map/all_gather | solution.py:64
  189.9 2.3 fusion.49
  192.5 21.7 %all_to_all.110 = f32[16,1,4096]{2,1,0:T(1,128)S(1)} all-to-all(f32[16,1,4096]{2,1,0:T(1,128)S(1)} %reshape.132), channel_id=1, replica_groups=mesh['tm'=32,'tile'=16] {'tile'}, dimensions={0} | all-to-all | bytes 524288 | tf_op jit(solution)/shard_map/all_to_all | solution.py:68
  218.7 2.5 collective-permute-done
  222.4 100.3 %all_to_all.111 = bf16[16,64,1024]{2,1,0:T(8,128)(2,1)S(1)} all-to-all(bf16[16,64,1024]{2,1,0:T(8,128)(2,1)S(1)} %tile.12), channel_id=1, replica_groups=mesh['tm'=32,'tile'=16] {'tile'}, dimensions={0} | all-to-all | bytes 4194304 | tf_op jit(solution)/shard_map/all_to_all | solution.py:14
  325.2 72.1 %all-gather.10.cloned.1.call-done = bf16[1024,1024]{1,0:T(8,128)(2,1)} async-done(((bf16[64,1024]{1,0:T(8,128)(2,1)}), bf16[1024,1024]{1,0:T(8,128)(2,1)}) %all-gather.10.cloned.1.call-update) | async-done | bytes 2097168 | tf_op jit(solution)/shard_map/all_gather | solution.py:64
  397.3 2.3 fusion.47
  400.6 21.8 %all_to_all.112 = f32[16,1,4096]{2,1,0:T(1,128)S(1)} all-to-all(f32[16,1,4096]{2,1,0:T(1,128)} %reshape.134), channel_id=1, replica_groups=mesh['tm'=32,'tile'=16] {'tile'}, dimensions={0} | all-to-all | bytes 524288 | tf_op jit(solution)/shard_map/all_to_all | solution.py:68
  430.5 2.8 collective-permute-done.1
  433.6 97.7 %all_to_all.113 = bf16[16,64,1024]{2,1,0:T(8,128)(2,1)S(1)} all-to-all(bf16[16,64,1024]{2,1,0:T(8,128)(2,1)S(1)} %tile.13), channel_id=1, replica_groups=mesh['tm'=32,'tile'=16] {'tile'}, dimensions={0} | all-to-all | bytes 4194304 | tf_op jit(solution)/shard_map/all_to_all | solution.py:14
  533.8 74.5 %all-gather.12.cloned.1.call-done = bf16[1024,1024]{1,0:T(8,128)(2,1)} async-done(((bf16[64,1024]{1,0:T(8,128)(2,1)}), bf16[1024,1024]{1,0:T(8,128)(2,1)}) %all-gather.12.cloned.1.call-update) | async-done | bytes 2097168 | tf_op jit(solution)/shard_map/all_gather | solution.py:64
  608.3 3.1 fusion.45
  611.4 2.1 reshape.136
  613.4 22.1 %all_to_all.114 = f32[16,1,4096]{2,1,0:T(1,128)} all-to-all(f32[16,1,4096]{2,1,0:T(1,128)} %reshape.136), channel_id=1, replica_groups=mesh['tm'=32,'tile'=16] {'tile'}, dimensions={0} | all-to-all | bytes 524288 | tf_op jit(solution)/shard_map/all_to_all | solution.py:68
  635.5 2.9 reduce.2
  638.4 1.9 reshape.137
  640.4 2.2 copy.31
  648.0 2.8 collective-permute-done.2
  652.0 102.9 %all_to_all.115 = bf16[16,64,1024]{2,1,0:T(8,128)(2,1)S(1)} all-to-all(bf16[16,64,1024]{2,1,0:T(8,128)(2,1)S(1)} %tile.14), channel_id=1, replica_groups=mesh['tm'=32,'tile'=16] {'tile'}, dimensions={0} | all-to-all | bytes 4194304 | tf_op jit(solution)/shard_map/all_to_all | solution.py:14
  759.6 32.0 %all-reduce = bf16[1024]{0:T(1024)(128)(2,1)S(1)} all-reduce(bf16[1024]{0:T(1024)(128)(2,1)S(1)} %dynamic-update-slice), channel_id=2, replica_groups=mesh['tm'=32,'tile'=16] {'tile'}, use_global_device_ids=true, to_apply=%add | all-reduce | flops 1024 | bytes 4096 | tf_op jit(solution)/shard_map/all_gather | solution.py:53
  791.8 2.1 collective-permute-start.3
  795.2 27.0 %all-reduce.1 = bf16[1024]{0:T(1024)(128)(2,1)S(1)} all-reduce(bf16[1024]{0:T(1024)(128)(2,1)S(1)} %dynamic-update-slice.1), channel_id=1, replica_groups=mesh['tm'=32,'tile'=16] {'tile'}, use_global_device_ids=true, to_apply=%add.1 | all-reduce | flops 1024 | bytes 4096
  822.4 1.9 collective-permute-start.4
  825.9 29.1 %all-reduce.2 = bf16[1024]{0:T(1024)(128)(2,1)S(1)} all-reduce(bf16[1024]{0:T(1024)(128)(2,1)S(1)} %dynamic-update-slice.2), channel_id=1, replica_groups=mesh['tm'=32,'tile'=16] {'tile'}, use_global_device_ids=true, to_apply=%add.2 | all-reduce | flops 1024 | bytes 4096
  855.1 1.9 collective-permute-start.5
  858.5 27.0 %all-reduce.3 = bf16[1024]{0:T(1024)(128)(2,1)S(1)} all-reduce(bf16[1024]{0:T(1024)(128)(2,1)S(1)} %dynamic-update-slice.3), channel_id=1, replica_groups=mesh['tm'=32,'tile'=16] {'tile'}, use_global_device_ids=true, to_apply=%add.3 | all-reduce | flops 1024 | bytes 4096
  887.3 28.3 %all-gather.1 = f32[16,64,8]{1,2,0:T(8,128)S(1)} all-gather(f32[1,64,8]{1,2,0:T(8,128)S(1)} %bitcast.168), channel_id=1, replica_groups=mesh['tm'=32,'tile'=16] {'tile'}, dimensions={0}, use_global_device_ids=true | all-gather | bytes 34816 | tf_op jit(solution)/shard_map/all_gather | solution.py:89
  920.3 2.3 fusion.43
  923.6 5.5 all-to-all-start.7
  929.2 3.8 fusion
  933.0 30.1 %all-gather.2 = f32[16,64,8]{1,2,0:T(8,128)S(1)} all-gather(f32[1,64,8]{1,2,0:T(8,128)S(1)} %bitcast.169), channel_id=1, replica_groups=mesh['tm'=32,'tile'=16] {'tile'}, dimensions={0}, use_global_device_ids=true | all-gather | bytes 34816 | tf_op jit(solution)/shard_map/all_gather | solution.py:90
  (126 shorter events, 49.2 us)
Async XLA Ops:
  7.2 112.8 %copy-start = (bf16[1,64,1024]{2,1,0:T(8,128)(2,1)S(1)}, bf16[1,64,1024]{2,1,0:T(8,128)(2,1)}, u32[]{:S(2)}) copy-start(bf16[1,64,1024]{2,1,0:T(8,128)(2,1)} %param.12) | copy-start | bytes 393220
  7.2 182.7 %all-gather.8.cloned.1.call-start = ((), (), s32[]{:S(2)}) async-start(), calls=%async_computation.8 | async-start | bytes 2228224 | tf_op jit(solution)/shard_map/all_gather | solution.py:64
  121.1 276.2 %all-gather.10.cloned.1.call-start = ((), (), s32[]{:S(2)}) async-start(), calls=%async_computation.9 | async-start | bytes 2228224 | tf_op jit(solution)/shard_map/all_gather | solution.py:64
  192.2 24.5 %copy-start.4 = (bf16[1,64,1024]{2,1,0:T(8,128)(2,1)S(1)}, bf16[1,64,1024]{2,1,0:T(8,128)(2,1)}, u32[]{:S(2)}) copy-start(bf16[1,64,1024]{2,1,0:T(8,128)(2,1)} %param.14) | copy-start | bytes 393220
  216.8 4.4 collective-permute-start
  322.7 1.3 copy-start.1
  325.2 283.1 %all-gather.12.cloned.1.call-start = ((), (), s32[]{:S(2)}) async-start(), calls=%async_computation.10 | async-start | bytes 2228224 | tf_op jit(solution)/shard_map/all_gather | solution.py:64
  428.6 4.7 collective-permute-start.1
  433.3 97.9 %copy-start.5 = (bf16[64,1024]{1,0:T(8,128)(2,1)}, bf16[64,1024]{1,0:T(8,128)(2,1)S(1)}, u32[]{:S(2)}) copy-start(bf16[64,1024]{1,0:T(8,128)(2,1)S(1)} %broadcast_select_fusion.1) | copy-start | bytes 393220
  531.3 1.3 copy-start.2
  533.7 386.5 %all-gather.14.cloned.1.call-start = ((), (), s32[]{:S(2)}) async-start(), calls=%async_computation.11 | async-start | bytes 2228224 | tf_op jit(solution)/shard_map/all_gather | solution.py:64
  613.4 37.4 %copy-start.6 = (bf16[64,1024]{1,0:T(8,128)(2,1)S(1)}, bf16[64,1024]{1,0:T(8,128)(2,1)}, u32[]{:S(2)}) copy-start(bf16[64,1024]{1,0:T(8,128)(2,1)} %copy-done.5) | copy-start | bytes 393220
  646.1 4.7 collective-permute-start.2
  754.9 1.3 copy-start.3
  754.9 4.4 copy-start.16
  754.9 36.8 %copy-start.19 = (f32[1,64]{1,0:T(1,128)S(1)}, f32[1,64]{1,0:T(1,128)}, u32[]{:S(2)}) copy-start(f32[1,64]{1,0:T(1,128)} %param.13) | copy-start | bytes 772
  754.9 69.5 %copy-start.18 = (s32[8]{0:T(128)S(1)}, s32[8]{0:T(128)}, u32[]{:S(2)}) copy-start(s32[8]{0:T(128)} %param.21) | copy-start | bytes 100
  754.9 102.1 %copy-start.15 = (s32[8,4]{0,1:T(4,128)S(1)}, s32[8,4]{0,1:T(4,128)}, u32[]{:S(2)}) copy-start(s32[8,4]{0,1:T(4,128)} %param.20) | copy-start | bytes 388
  754.9 132.4 %copy-start.13 = (f32[8,64]{1,0:T(8,128)S(1)}, f32[8,64]{1,0:T(8,128)}, u32[]{:S(2)}) copy-start(f32[8,64]{1,0:T(8,128)} %param.18) | copy-start | bytes 6148
  756.2 160.1 %copy-start.10 = (f32[8,4,128]{2,1,0:T(4,128)S(1)}, f32[8,4,128]{2,1,0:T(4,128)}, u32[]{:S(2)}) copy-start(f32[8,4,128]{2,1,0:T(4,128)} %param.22) | copy-start | bytes 49156
  791.8 3.2 collective-permute-start.3
  822.4 3.2 collective-permute-start.4
  855.1 3.2 collective-permute-start.5
  887.3 35.2 %copy-start.11 = (f32[8,64]{1,0:T(8,128)}, f32[8,64]{1,0:T(8,128)S(1)}, u32[]{:S(2)}) copy-start(f32[8,64]{1,0:T(8,128)S(1)} %add.74) | copy-start | bytes 6148
  923.6 40.4 %all-to-all-start.7 = ((f32[16,1,4096]{2,1,0:T(1,128)}), f32[16,1,4096]{2,1,0:T(1,128)S(1)}, u32[]{:S(2)}, u32[]{:S(2)}) async-start(f32[16,1,4096]{2,1,0:T(1,128)} %reshape.138), calls=%async_computation.7 | async-start | bytes 524288 | tf_op jit(solution)/shard_map/all_to_all | solution.py:68
  929.1 3.8 copy-start.14
  929.2 34.0 %copy-start.17 = (f32[1024]{0:T(1024)S(1)}, f32[1024]{0:T(1024)}, u32[]{:S(2)}) copy-start(f32[1024]{0:T(1024)} %param.23) | copy-start | bytes 12292
  932.9 33.1 %copy-start.7 = (f32[1,64,1024]{2,1,0:T(8,128)S(1)}, f32[1,64,1024]{2,1,0:T(8,128)}, u32[]{:S(2)}) copy-start(f32[1,64,1024]{2,1,0:T(8,128)} %all_to_all.100) | copy-start | bytes 786436
  933.0 33.1 %copy-start.8 = (f32[1,64,1024]{2,1,0:T(8,128)S(1)}, f32[1,64,1024]{2,1,0:T(8,128)}, u32[]{:S(2)}) copy-start(f32[1,64,1024]{2,1,0:T(8,128)} %all_to_all.99) | copy-start | bytes 786436
  933.0 33.1 %copy-start.9 = (f32[1,64,1024]{2,1,0:T(8,128)S(1)}, f32[1,64,1024]{2,1,0:T(8,128)}, u32[]{:S(2)}) copy-start(f32[1,64,1024]{2,1,0:T(8,128)} %all_to_all.98) | copy-start | bytes 786436
  933.0 33.8 %copy-start.12 = (f32[8,64]{1,0:T(8,128)}, f32[8,64]{1,0:T(8,128)S(1)}, u32[]{:S(2)}) copy-start(f32[8,64]{1,0:T(8,128)S(1)} %add.75) | copy-start | bytes 6148
Sparse Core Ops, SparseCore 0:
  121.2 68.6 all-gather.7
  325.3 71.9 all-gather.9
  533.9 74.3 all-gather.11
  757.5 69.1 all-gather.13
